TPU v7x, 256 devices: a whole 4x4x8 slice. The times are simulated.
256 devices in a mesh: img: 8 (over z_lo, core), txt: 32 (over x, y, z_hi).
Axes of the slice: x: 4, y: 4, z: 8 (z_hi: 2, z_lo: 4; z = z_hi * 4 + z_lo), core: 2. Of those that a mesh axis runs over, the one named last changes fastest.
Arguments:
- images: float32 [22528, 1152], P(('img', 'txt')), may hold values from -0.18 to 0.18
- texts: float32 [22528, 1152], P(('txt', 'img')), may hold values from -0.18 to 0.18
- scale: float32 [1], replicated, may hold values from 5 to 20
- bias: float32 [1], replicated, may hold values from -3 to -1
Outputs:
- loss: float32 [1], replicated
- image_grad: float32 [22528, 1152], P(('img', 'txt'))
- text_grad: float32 [22528, 1152], P(('txt', 'img'))
All inputs are finite; a program needn't handle non-finite values.
Results may differ from a plain program's by a relative error of at most 0.0006.
The roundings to bfloat16 on the way count: a program that leaves them out, or rounds other values in their place, can miss the bound.
Values may be sent and summed in bfloat16 or wider, within the bound.
No kernel may reach another device: no remote copies, remote signals or barrier semaphores. Data moves between devices by JAX's collectives and lax.ppermute only.
A program may use at most 128 MiB of HBM per device.

v0:
```python
import jax
import jax.numpy as jnp
from jax import lax
from jax.sharding import PartitionSpec as P


def unit_rows(x):
    norm = jnp.sqrt(jnp.sum(x * x, axis=1, keepdims=True) + 1e-06)
    return (x / norm, norm)


def project_back(grad_unit, unit, norm):
    return (grad_unit - unit * jnp.sum(unit * grad_unit, axis=1, keepdims=True)) / norm


def on_device(images, texts, scale, bias):
    factor = scale[0]
    offset = bias[0]
    own = images.shape[0]
    n_img = lax.axis_size("img")
    n_txt = lax.axis_size("txt")
    img_pos = lax.axis_index("img")
    txt_pos = lax.axis_index("txt")
    unit_img, img_norm = unit_rows(images)
    unit_txt, txt_norm = unit_rows(texts)
    img_low = unit_img.astype(jnp.bfloat16)
    txt_low = unit_txt.astype(jnp.bfloat16)
    img_whole = lax.all_gather(img_low, "txt", axis=0, tiled=True)
    txt_whole = lax.all_gather(txt_low, "img", axis=0, tiled=True)
    row_ids = img_pos * img_whole.shape[0] + jnp.arange(img_whole.shape[0], dtype=jnp.int32)
    col_ids = txt_pos * txt_whole.shape[0] + jnp.arange(txt_whole.shape[0], dtype=jnp.int32)
    logits = (
        factor
        * lax.dot_general(
            img_whole, txt_whole, (((1,), (1,)), ((), ())), preferred_element_type=jnp.float32
        )
        + offset
    )
    label = (row_ids[:, None] == col_ids[None, :]).astype(jnp.float32)
    loss_part = jnp.sum(jax.nn.softplus(logits)) - jnp.sum(label * logits)
    coef = (jax.nn.sigmoid(logits) - label).astype(jnp.bfloat16)
    txt_grad_unit = lax.psum_scatter(
        factor
        * lax.dot_general(
            coef, img_whole, (((0,), (0,)), ((), ())), preferred_element_type=jnp.float32
        ),
        "img",
        scatter_dimension=0,
        tiled=True,
    )
    img_grad_unit = lax.psum_scatter(
        factor * jnp.dot(coef, txt_whole, preferred_element_type=jnp.float32),
        "txt",
        scatter_dimension=0,
        tiled=True,
    )
    text_grad = project_back(txt_grad_unit, unit_txt, txt_norm)
    image_grad = project_back(img_grad_unit, unit_img, img_norm)
    pairs_all = own * n_img * n_txt
    summed = lax.psum(loss_part, ("img", "txt"))
    loss = (summed / (pairs_all * pairs_all)).reshape(1)
    return (loss, image_grad, text_grad)


def solution(mesh):
    in_specs = (P(("img", "txt"), None), P(("txt", "img"), None), P(), P())
    out_specs = (P(), P(("img", "txt"), None), P(("txt", "img"), None))
    return jax.shard_map(
        on_device, mesh=mesh, in_specs=in_specs, out_specs=out_specs, check_vma=False
    )
```

profile of v0, /device:TPU:24, one launch (start us, length us, event | category | flops | bytes accessed | tf_op | source)
XLA Modules:
  0.0 589.4 jit_solution(15003680761668363641)
XLA Ops:
  7.2 0.0 all-gather.5.cloned.1.call-start
  7.2 1.1 multiply_reduce_fusion.2
  8.4 1.8 fusion.5
  10.1 0.0 all-gather.5.cloned.1.call-update
  10.2 0.0 all-gather.3.cloned.1.call-start
  10.2 1.1 multiply_reduce_fusion.3
  11.4 1.8 fusion.4
  13.2 0.0 all-gather.3.cloned.1.call-update
  13.2 0.0 reduce-scatter.10.cloned.1.call-start
  14.5 36.7 %all-gather.5.cloned.1.call-done = bf16[704,1152]{1,0:T(8,128)(2,1)} async-done(((bf16[88,1152]{1,0:T(8,128)(2,1)}), bf16[704,1152]{1,0:T(8,128)(2,1)}) %all-gather.5.cloned.1.call-update) | async-done | bytes 1622032 | tf_op jit(solution)/shard_map/all_gather | solution.py:29
  51.2 137.3 %all-gather.3.cloned.1.call-done = bf16[2816,1152]{1,0:T(8,128)(2,1)} async-done(((bf16[88,1152]{1,0:T(8,128)(2,1)}), bf16[2816,1152]{1,0:T(8,128)(2,1)}) %all-gather.3.cloned.1.call-update) | async-done | bytes 6488080 | tf_op jit(solution)/shard_map/all_gather | solution.py:28
  188.6 0.0 copy-start.2
  188.6 13.8 %fusion = (f32[]{:T(128)}, f32[]{:T(128)}, f32[2816,704]{0,1:T(8,128)S(1)}) fusion(s32[2816]{0:T(1024)S(1)} %iota_add_fusion, f32[]{:T(128)} %bitcast.14, f32[]{:T(128)} %bitcast.9, s32[704]{0:T(1024)S(1)} %iota_add_fusion.1, bf16[2816,1152]{1,0:T(8,128)(2,1)} %all-gather.3.cloned.1.call-done, bf16[704,1152]{1,0:T(8,128)(2,1)} %all-gather.5.cloned.1.call-done), kind=kOutput, calls=%fused_computation.4 | convolution fusion | flops 4591386624 | bytes 16054032 | tf_op jit(solution)/shard_map/dot_general | solution.py:34
  202.4 0.0 copy-start.4
  202.4 3.1 copy-done.4
  205.4 0.0 copy-done.2
  205.5 0.0 copy-start.3
  205.5 8.7 %convolution_multiply_fusion.1 = f32[704,1152]{1,0:T(8,128)} fusion(bf16[2816,1152]{1,0:T(8,128)(2,1)S(1)} %copy-done.2, f32[]{:T(128)} %bitcast.11, f32[2816,704]{0,1:T(8,128)S(1)} %get-tuple-element.5, s32[2816]{0:T(1024)S(1)} %iota_add_fusion, f32[]{:T(128)} %bitcast.13, s32[704]{0:T(1024)S(1)} %iota_add_fusion.1), kind=kOutput, calls=%fused_computation.9 | convolution fusion | flops 4586250240 | bytes 17676040 | tf_op jit(solution)/shard_map/dot_general | solution.py:44
  214.1 0.0 reduce-scatter.10.cloned.1.call-update
  214.2 0.0 reduce-scatter.8.cloned.1.call-start
  214.2 0.0 copy-done.3
  214.2 11.9 %convolution_multiply_fusion = f32[2816,1152]{1,0:T(8,128)} fusion(bf16[704,1152]{1,0:T(8,128)(2,1)S(1)} %copy-done.3, f32[]{:T(128)} %bitcast.10, f32[2816,704]{0,1:T(8,128)} %copy-done.4, s32[2816]{0:T(1024)S(1)} %iota_add_fusion, f32[]{:T(128)} %bitcast.12, s32[704]{0:T(1024)S(1)} %iota_add_fusion.1), kind=kOutput, calls=%fused_computation.1 | convolution fusion | flops 4588683264 | bytes 22542088 | tf_op jit(solution)/shard_map/dot_general | solution.py:52
  226.1 0.0 copy-start
  226.1 0.0 copy-start.1
  226.1 0.0 reduce-scatter.8.cloned.1.call-update
  227.5 77.0 %psum.7 = f32[]{:T(128)} all-reduce(f32[]{:T(128)S(6)} %sub.12), channel_id=1, replica_groups=mesh['img'=8,'txt'=32] {'img','txt'}, use_global_device_ids=true, to_apply=%region_4.5 | all-reduce | flops 1 | bytes 8 | tf_op jit(solution)/shard_map/psum | solution.py:60
  305.1 0.0 reduce-scatter.10.cloned.1.call-done
  305.2 0.0 copy-done
  305.2 1.2 multiply_reduce_fusion
  306.4 1.9 subtract_divide_fusion
  308.3 270.3 %reduce-scatter.8.cloned.1.call-done = f32[88,1152]{1,0:T(8,128)} async-done(((f32[2816,1152]{1,0:T(8,128)}), f32[88,1152]{1,0:T(8,128)}) %reduce-scatter.8.cloned.1.call-update) | async-done | bytes 405520
  578.6 0.0 copy-done.1
  578.6 1.2 multiply_reduce_fusion.1
  579.9 1.9 subtract_divide_fusion.1
  (4 shorter events, 0.0 us)
Async XLA Ops:
  7.2 44.1 %all-gather.5.cloned.1.call-start = ((), (), s32[]{:S(2)}) async-start(), calls=%async_computation.3 | async-start | bytes 1824768 | tf_op jit(solution)/shard_map/all_gather | solution.py:29
  10.2 178.4 %all-gather.3.cloned.1.call-start = ((), (), s32[]{:S(2)}) async-start(), calls=%async_computation.2 | async-start | bytes 6690816 | tf_op jit(solution)/shard_map/all_gather | solution.py:28
  13.2 292.0 %reduce-scatter.10.cloned.1.call-start = ((), (), s32[]{:S(2)}) async-start(), calls=%async_computation.5 | async-start | bytes 3649536
  188.6 16.9 %copy-start.2 = (bf16[2816,1152]{1,0:T(8,128)(2,1)S(1)}, bf16[2816,1152]{1,0:T(8,128)(2,1)}, u32[]{:S(2)}) copy-start(bf16[2816,1152]{1,0:T(8,128)(2,1)} %all-gather.3.cloned.1.call-done) | copy-start | bytes 19464196
  202.4 3.1 copy-start.4
  205.5 8.8 %copy-start.3 = (bf16[704,1152]{1,0:T(8,128)(2,1)S(1)}, bf16[704,1152]{1,0:T(8,128)(2,1)}, u32[]{:S(2)}) copy-start(bf16[704,1152]{1,0:T(8,128)(2,1)} %all-gather.5.cloned.1.call-done) | copy-start | bytes 4866052
  214.2 364.5 %reduce-scatter.8.cloned.1.call-start = ((), (), s32[]{:S(2)}) async-start(), calls=%async_computation.4 | async-start | bytes 13381632
  226.1 79.0 %copy-start = (f32[88,1152]{1,0:T(8,128)S(1)}, f32[88,1152]{1,0:T(8,128)}, u32[]{:S(2)}) copy-start(f32[88,1152]{1,0:T(8,128)} %param.5) | copy-start | bytes 1216516
  226.1 352.5 %copy-start.1 = (f32[88,1152]{1,0:T(8,128)S(1)}, f32[88,1152]{1,0:T(8,128)}, u32[]{:S(2)}) copy-start(f32[88,1152]{1,0:T(8,128)} %param.4) | copy-start | bytes 1216516
Sparse Core Ops, SparseCore 0:
  10.4 40.8 all-gather.4
  55.3 133.2 all-gather.2
  214.3 41.3 reduce-scatter.9
  262.3 316.2 reduce-scatter.7
where the time goes:
time: 591 us; the launch traced here: 589 us
  waiting for transfers between devices  444 us (75%)
  blocking collectives  77 us (13%)
  matrix products  34.4 us (6%)
  between operations  18.3 us (3%)
  other arithmetic  12.1 us (2%)
    unnamed x6, waiting for transfers between devices  270 us
    all_gather x1, waiting for transfers between devices, on_device(): img_whole = lax.all_gather(img_low, 'txt', axis=0, tiled=True)  137 us
    psum x1, blocking collectives, on_device(): summed = lax.psum(loss_part, ('img', 'txt'))  77 us
    all_gather x1, waiting for transfers between devices, on_device(): txt_whole = lax.all_gather(txt_low, 'img', axis=0, tiled=True)  36.7 us
    dot_general x1, matrix products, on_device(): lax.dot_general(img_whole, txt_whole, (((1,), (1,)), ((), ())), preferred...  13.8 us
    dot_general x1, matrix products, on_device(): jnp.dot(coef, txt_whole, preferred_element_type=jnp.float32)  11.9 us
  transfers between devices with their start and end apart: 4, of which 3 were waited for; matrix products, arithmetic and copies ran while one was open for 3% of the time, Pallas kernels for 0%

commit v1 on v0

v1 whole, which is shorter than its diff:
```python
import jax
import jax.numpy as jnp
import numpy as np
from jax import lax
from jax.experimental import pallas as pl
from jax.experimental.pallas import tpu as pltpu
from jax.sharding import Mesh
from jax.sharding import PartitionSpec as P

AXES = ("zl", "c", "x", "y", "zh")
SIZES = (4, 2, 4, 4, 2)
NX, NY, NZ = 4, 4, 8
OWN = 88
BLK = 2 * OWN
D = 1152
M = 16 * OWN
PAIRS = 22528
F16 = jnp.float16
F32 = jnp.float32
BF16 = jnp.bfloat16


def linear(x, y, z, c):
    return int(np.ravel_multi_index((z % 4, c, x, y, z // 4), SIZES))


def pairs_of(move):
    pairs = []
    for x in range(NX):
        for y in range(NY):
            for z in range(NZ):
                for c in (0, 1):
                    to = move(x, y, z, c)
                    pairs.append((linear(x, y, z, c), linear(*to)))
    return pairs


def along_first(step):
    return pairs_of(
        lambda x, y, z, c: ((x + step) % NX, y, z, c) if c == 0 else (x, (y + step) % NY, z, c)
    )


def along_second(step):
    return pairs_of(
        lambda x, y, z, c: (x, (y + step) % NY, z, c) if c == 0 else ((x + step) % NX, y, z, c)
    )


def along_z(step):
    return pairs_of(lambda x, y, z, c: (x, y, (z + step) % NZ, c))


def other_core():
    return pairs_of(lambda x, y, z, c: (x, y, z, 1 - c))


def send(value, pairs):
    return lax.ppermute(value, AXES, pairs)


def normalize_kernel(img_ref, txt_ref, *out_refs):
    for k, ref in enumerate((img_ref, txt_ref)):
        v = ref[...]
        norm = jnp.sqrt(jnp.sum(v * v, axis=1, keepdims=True) + 1e-06)
        out_refs[k][...] = (v / norm).astype(BF16)


def normalize(images, texts):
    return pl.pallas_call(
        normalize_kernel,
        out_shape=(jax.ShapeDtypeStruct((OWN, D), BF16),) * 2,
        name="normalize",
    )(images, texts)


def project_kernel(sc_ref, lean_ref, img_ref, txt_ref, gi_ref, gt_ref, oi_ref, ot_ref):
    factor = sc_ref[0]
    lean = lean_ref[0] * 16.0
    for v_ref, g_ref, o_ref in ((img_ref, gi_ref, oi_ref), (txt_ref, gt_ref, ot_ref)):
        v = v_ref[...]
        norm = jnp.sqrt(jnp.sum(v * v, axis=1, keepdims=True) + 1e-06)
        unit = v / norm
        g = factor * (g_ref[...] + lean * unit.astype(BF16).astype(F32))
        o_ref[...] = (g - unit * jnp.sum(unit * g, axis=1, keepdims=True)) / norm


def project(scale, lean, images, texts, gi, gt):
    smem = pl.BlockSpec(memory_space=pltpu.SMEM)
    vmem = pl.BlockSpec(memory_space=pltpu.VMEM)
    out = jax.ShapeDtypeStruct((OWN, D), F32)
    return pl.pallas_call(
        project_kernel,
        out_shape=(out, out),
        in_specs=[smem, smem, vmem, vmem, vmem, vmem],
        out_specs=(vmem, vmem),
        name="project",
    )(scale, lean, images, texts, gi, gt)


LINE = (0, -1, 1, 2)
ACROSS = (0, 1, -1, 2)
TXT_AT = (0, -1, 1, 4, 2, -3, -2, 3)
BLOCKS = 16


def block_ids():
    x, y, c = (lax.axis_index(name) for name in ("x", "y", "c"))
    zl, zh = lax.axis_index("zl"), lax.axis_index("zh")
    z = zh * 4 + zl
    imgs, txts = [], []
    for b in ACROSS:
        for a in LINE:
            px = lax.rem(x + jnp.where(c == 0, a % NX, b % NX), NX)
            py = lax.rem(y + jnp.where(c == 0, b % NY, a % NY), NY)
            imgs.append((((zl * 2 + c) * NX + px) * NY + py) * 2 + zh)
    for k in (c, 1 - c):
        for dz in TXT_AT:
            pz = lax.rem(z + dz % NZ, NZ)
            txts.append(((x * NY + y) * 2 + lax.div(pz, 4)) * 8 + lax.rem(pz, 4) * 2 + k)
    return imgs, txts


ROWS = 4 * OWN
HALF = M // 2


def spread(ids, shape, dim):
    at = lax.broadcasted_iota(jnp.int32, shape, dim)
    rows = jnp.zeros(shape, jnp.int32)
    for k, block in enumerate(ids):
        rows = jnp.where(at >= k * OWN, (block - k) * OWN, rows)
    return rows + at


def load_all(parts, whole, sem):
    loads = []
    at = 0
    for k, ref in enumerate(parts):
        n = ref.shape[0]
        loads.append(pltpu.make_async_copy(ref, whole.at[pl.ds(at, n)], sem.at[k]))
        at += n
    for load in loads:
        load.start()
    return loads


def img_grad(coef, img, txt, at, lean):
    g = jnp.dot(coef[at, :], txt[...], preferred_element_type=F32)
    return g - lean * img[at, :].astype(F32)


def txt_grad(coef, img, txt, start, size, lean):
    g = lax.dot_general(
        coef[:, start : start + size], img[...], (((0,), (0,)), ((), ())), preferred_element_type=F32
    )
    return g - lean * txt[pl.ds(start, size), :].astype(F32)


def score_kernel(sc_ref, bi_ref, lean_ref, *refs):
    imgs, txts = refs[:4], refs[4:10]
    coef_ref, gw_ref, gu_ref, gd_ref = refs[10:14]
    img, txt, coef, gt, last, img_sem, txt_sem, out_sem = refs[14:]
    factor = sc_ref[0] * LOG2E
    offset = bi_ref[0] * LOG2E
    lean = lean_ref[0]
    loads = load_all(txts, txt, txt_sem) + load_all(imgs, img, img_sem)
    img_ids, txt_ids = block_ids()
    cid = spread(txt_ids, (1, M), 1)
    for load in loads:
        load.wait()
    total = jnp.zeros((8, M), F32)
    stores = []

    def keep(src, dst):
        store = pltpu.make_async_copy(src, dst, out_sem.at[len(stores)])
        store.start()
        stores.append(store)

    for k in range(M // ROWS):
        at = pl.ds(k * ROWS, ROWS)
        s = lax.dot_general(
            img[at, :], txt[...], (((1,), (1,)), ((), ())), preferred_element_type=F32
        )
        x = s * factor + offset
        e = jnp.exp2(x)
        u = 1.0 + e
        r = 1.0 / u
        label = spread(img_ids[4 * k : 4 * k + 4], (ROWS, 1), 0) == cid
        coef[at, :] = jnp.where(label, -r, e * r).astype(BF16)
        four = u.reshape(ROWS // 32, 4, 8, M)
        four = (four[:, 0] * four[:, 1]) * (four[:, 2] * four[:, 3])
        total = total + jnp.sum(jnp.log2(four), axis=0)
        total = total - jnp.sum(jnp.where(label, x, 0.0).reshape(ROWS // 8, 8, M), axis=0)
        keep(coef.at[at], coef_ref.at[at])
    part = total[:, :128]
    for k in range(1, M // 128):
        part = part + total[:, k * 128 : (k + 1) * 128]
    last[...] = jnp.zeros((8, D), F32)
    last[:, :128] = part * LN2
    keep(last, gw_ref.at[pl.ds(HALF, 8)])
    at = pl.ds(0, HALF)
    gt[at, :] = txt_grad(coef, img, txt, HALF, HALF, lean)
    keep(gt.at[at], gw_ref.at[at])
    at = pl.ds(HALF, ROWS)
    gt[at, :] = txt_grad(coef, img, txt, ROWS, ROWS, lean)
    keep(gt.at[pl.ds(HALF, BLK)], gu_ref)
    keep(gt.at[pl.ds(HALF + BLK, BLK)], gd_ref)
    for store in stores:
        store.wait()


LOG2E = 1.4426950408889634
LN2 = 0.6931471805599453
SMEM = pl.BlockSpec(memory_space=pltpu.SMEM)
VMEM = pl.BlockSpec(memory_space=pltpu.VMEM)
ANY = pl.BlockSpec(memory_space=pl.ANY)


def f32(rows):
    return jax.ShapeDtypeStruct((rows, D), F32)


def score(scale, bias, lean, imgs, txts):
    return pl.pallas_call(
        score_kernel,
        out_shape=(
            jax.ShapeDtypeStruct((M, M), BF16),
            f32(HALF + 8),
            f32(BLK),
            f32(BLK),
        ),
        in_specs=[SMEM] * 3 + [ANY] * 10,
        out_specs=(ANY,) * 4,
        scratch_shapes=[
            pltpu.VMEM((M, D), BF16),
            pltpu.VMEM((M, D), BF16),
            pltpu.VMEM((M, M), BF16),
            pltpu.VMEM((3 * ROWS, D), F32),
            pltpu.VMEM((8, D), F32),
            pltpu.SemaphoreType.DMA((4,)),
            pltpu.SemaphoreType.DMA((6,)),
            pltpu.SemaphoreType.DMA((M // ROWS + 4,)),
        ],
        compiler_params=pltpu.CompilerParams(vmem_limit_bytes=48 * 2**20),
        cost_estimate=pl.CostEstimate(
            flops=4 * M * M * D, bytes_accessed=12 * M * D, transcendentals=3 * M * M
        ),
        name="score",
    )(scale, bias, lean, *imgs, *txts)


def across_kernel(lean_ref, coef_ref, *refs):
    imgs, txts, out_refs = refs[:3], refs[3:9], refs[9:12]
    img, txt, coef, gi, img_sem, txt_sem, coef_sem, out_sem = refs[12:]
    lean = lean_ref[0]
    loads = [pltpu.make_async_copy(coef_ref.at[pl.ds(ROWS, 3 * ROWS)], coef, coef_sem)]
    loads[0].start()
    loads += load_all(txts, txt, txt_sem) + load_all(imgs, img, img_sem)
    for load in loads:
        load.wait()
    stores = []
    for k, dst in enumerate(out_refs):
        at = pl.ds(k * ROWS, ROWS)
        gi[at, :] = img_grad(coef, img, txt, at, lean)
        store = pltpu.make_async_copy(gi.at[at], dst, out_sem.at[k])
        store.start()
        stores.append(store)
    for store in stores:
        store.wait()


def across(lean, coef, imgs, txts):
    return pl.pallas_call(
        across_kernel,
        out_shape=(f32(ROWS),) * 3,
        in_specs=[SMEM] + [ANY] * 10,
        out_specs=(ANY,) * 3,
        scratch_shapes=[
            pltpu.VMEM((3 * ROWS, D), BF16),
            pltpu.VMEM((M, D), BF16),
            pltpu.VMEM((3 * ROWS, M), BF16),
            pltpu.VMEM((3 * ROWS, D), F32),
            pltpu.SemaphoreType.DMA((3,)),
            pltpu.SemaphoreType.DMA((6,)),
            pltpu.SemaphoreType.DMA,
            pltpu.SemaphoreType.DMA((3,)),
        ],
        compiler_params=pltpu.CompilerParams(vmem_limit_bytes=48 * 2**20),
        cost_estimate=pl.CostEstimate(
            flops=2 * 3 * ROWS * M * D, bytes_accessed=8 * M * D, transcendentals=0
        ),
        name="across",
    )(lean, coef, *imgs, *txts)


def near_kernel(lean_ref, coef_ref, *refs):
    imgs, txts, gl_ref, gf_ref = refs[:4], refs[4:10], refs[10], refs[11]
    img, txt, coef, gi, gt, img_sem, txt_sem, coef_sem, out_sem = refs[12:]
    lean = lean_ref[0]
    loads = [pltpu.make_async_copy(coef_ref, coef, coef_sem)]
    loads[0].start()
    loads += load_all(imgs, img, img_sem) + load_all(txts, txt, txt_sem)
    for load in loads:
        load.wait()
    gt[...] = txt_grad(coef, img, txt, 0, ROWS, lean)
    first = pltpu.make_async_copy(gt, gf_ref, out_sem.at[0])
    first.start()
    gi[...] = img_grad(coef, img, txt, pl.ds(0, ROWS), lean)
    second = pltpu.make_async_copy(gi, gl_ref, out_sem.at[1])
    second.start()
    first.wait()
    second.wait()


def nearby(lean, coef, imgs, txts):
    return pl.pallas_call(
        near_kernel,
        out_shape=(f32(ROWS),) * 2,
        in_specs=[SMEM] + [ANY] * 11,
        out_specs=(ANY,) * 2,
        scratch_shapes=[
            pltpu.VMEM((M, D), BF16),
            pltpu.VMEM((M, D), BF16),
            pltpu.VMEM((M, M), BF16),
            pltpu.VMEM((ROWS, D), F32),
            pltpu.VMEM((ROWS, D), F32),
            pltpu.SemaphoreType.DMA((4,)),
            pltpu.SemaphoreType.DMA((6,)),
            pltpu.SemaphoreType.DMA,
            pltpu.SemaphoreType.DMA((2,)),
        ],
        compiler_params=pltpu.CompilerParams(vmem_limit_bytes=48 * 2**20),
        cost_estimate=pl.CostEstimate(
            flops=M * M * D, bytes_accessed=12 * M * D, transcendentals=0
        ),
        name="nearby",
    )(lean, coef, *imgs, *txts)


def tie(*values):
    return lax.optimization_barrier(values)


def on_device(images, texts, scale, bias):
    middle = jax.nn.sigmoid(bias)
    low_end = jax.nn.sigmoid(bias - scale * np.float32(np.sqrt(3 / D)))
    high_end = jax.nn.sigmoid(bias + scale * np.float32(np.sqrt(3 / D)))
    slope = (2 / 3) * middle * (1 - middle)
    slope = slope + (1 / 6) * (low_end * (1 - low_end) + high_end * (1 - high_end))
    lean = scale * slope * np.float32(M / D)

    img, txt = normalize(images, texts)
    swap = other_core()

    t4 = send(txt, along_z(4))
    i_n, i_p = send(img, along_first(1)), send(img, along_first(-1))
    i2 = send(img, along_first(-2))
    tp = send(txt, along_z(-1))
    txt_late, i_n = tie(txt, i_n)
    tn = send(txt_late, along_z(1))
    line = jnp.concatenate([img, i_n, i_p, i2])
    qp, qn = send(line, along_second(-1)), send(line, along_second(1))
    line_late, tp = tie(line, tp)
    q2 = send(line_late, along_second(-2))
    up = send(jnp.concatenate([tp, t4]), along_z(-1))
    down = send(jnp.concatenate([tn, t4]), along_z(1))
    fan = jnp.concatenate([txt, tn, tp, t4])
    fan, qp = tie(fan, qp)
    fan_w = send(fan, swap)
    up_w, down_w = send(up, swap), send(down, swap)

    imgs = (line, qp, qn, q2)
    txts = (fan, up, down, fan_w, up_w, down_w)
    coef, gw, gup, gdown = score(scale, bias, lean, imgs, txts)

    def low16(v):
        return v.astype(F16)

    def wide(v):
        return v.astype(F32)

    def limbs(value):
        high = jnp.floor(value / 2048.0)
        rest = value - 2048.0 * high
        middle = jnp.floor(rest)
        last = jnp.floor((rest - middle) * 2048.0)
        return jnp.concatenate([high, middle, last], axis=1)

    def value_of(parts):
        return parts[:, :128] * 2048.0 + (parts[:, 128:256] + parts[:, 256:] / 2048.0)

    def tagged(rows, parts):
        return jnp.concatenate([low16(rows), low16(jnp.pad(parts, ((0, 0), (0, D - 384))))])

    def tag_of(message):
        return wide(message[-8:, :384])

    loss = gw[HALF:, :128]
    gw = send(gw, swap)
    loss = loss + gw[HALF:, :128]
    gp, gn, g2 = across(lean, coef, imgs[1:], txts)
    m_up = low16(gup + gw[ROWS : ROWS + BLK])
    m_down = low16(gdown + gw[ROWS + BLK : HALF])
    from_n = send(m_up, along_z(1))
    from_p = send(m_down, along_z(-1))
    tag = limbs(loss)
    r2 = send(tagged(g2, tag), along_second(2))
    rp = send(tagged(gp, tag), along_second(1))
    rn = send(tagged(gn, tag), along_second(-1))
    late, m_up, m_down, gn = tie(coef, m_up, m_down, gn)
    gline, gfan = nearby(lean, late, imgs, txts)
    gfan = gfan + gw[:ROWS]
    fan_4 = gfan[3 * OWN :] + wide(from_n[OWN:]) + wide(from_p[OWN:])
    fan_p = gfan[2 * OWN : 3 * OWN] + wide(from_n[:OWN])
    fan_n = gfan[OWN : 2 * OWN] + wide(from_p[:OWN])
    e4 = send(low16(fan_4), along_z(4))
    ep = send(low16(fan_p), along_z(1))
    en = send(low16(fan_n), along_z(-1))
    gline = gline + (wide(rp[:ROWS]) + wide(rn[:ROWS]) + wide(r2[:ROWS]))
    tag = limbs(value_of(tag + tag_of(rp) + tag_of(rn) + tag_of(r2)))
    d2 = send(tagged(gline[3 * OWN :], tag), along_first(2))
    dp = send(tagged(gline[2 * OWN : 3 * OWN], tag), along_first(1))
    dn = send(tagged(gline[OWN : 2 * OWN], tag), along_first(-1))
    loss = value_of(tag + tag_of(dp) + tag_of(dn) + tag_of(d2))
    loss = lax.all_to_all(jnp.tile(loss, (NZ, 1)), ("zh", "zl"), 0, 0, tiled=True)
    txt_sum = gfan[:OWN] + (wide(e4) + wide(ep) + wide(en))
    img_sum = gline[:OWN] + (wide(d2[:OWN]) + wide(dp[:OWN]) + wide(dn[:OWN]))
    image_grad, text_grad = project(scale, lean, images, texts, img_sum, txt_sum)
    loss = (jnp.sum(loss) / (PAIRS * PAIRS)).reshape(1)
    return (loss, image_grad, text_grad)


def solution(mesh):
    fine = Mesh(np.asarray(mesh.devices).reshape(SIZES), AXES)
    img = P(("zl", "c", "x", "y", "zh"), None)
    txt = P(("x", "y", "zh", "zl", "c"), None)
    return jax.shard_map(
        on_device,
        mesh=fine,
        in_specs=(img, txt, P(), P()),
        out_specs=(P(), img, txt),
        check_vma=False,
    )
```

time: 591 us -> 138 us (0.23)
  waiting for transfers between devices: 444 us -> 32.2 us
  blocking collectives: 77 us -> 0 us
  starting transfers between devices: 0.16 us -> 52.5 us
  matrix products: 34.4 us -> 0 us
  Pallas kernels: 0 us -> 32.1 us
  between operations: 18.3 us -> 4.24 us
    unnamed x6 -> x0, waiting for transfers between devices: 270 us -> none
    all_gather x2 -> x0, waiting for transfers between devices: 174 us -> none  [the longest x1 137 us: on_device(): img_whole = lax.all_gather(img_low, 'txt', axis=0, tiled=True)]
    psum x1 -> x0, blocking collectives: 77 us -> none  [on_device(): summed = lax.psum(loss_part, ('img', 'txt'))]
    ppermute x0 -> x26, starting transfers between devices: none -> 44 us  [send(): return lax.ppermute(value, AXES, pairs)]
    dot_general x3 -> x0, matrix products: 34.4 us -> none  [the longest x1 13.8 us: on_device(): lax.dot_general(img_whole, txt_whole, (((1,), (1,)), ((), ())), preferred...]
    pallas_call x0 -> x5, Pallas kernels: none -> 32.1 us  [the longest x1 13.2 us: score(): pl.pallas_call(score_kernel, out_shape=(jax.ShapeDtypeStruct((M, M), BF16...]
    ppermute x0 -> x26, waiting for transfers between devices: none -> 27.6 us  [send(): return lax.ppermute(value, AXES, pairs)]
    all_to_all x0 -> x1, starting transfers between devices: none -> 8.46 us  [on_device(): lax.all_to_all(jnp.tile(loss, (NZ, 1)), ('zh', 'zl'), 0, 0, tiled=True)]
  transfers between devices with their start and end apart: 4 -> 27, of which waited for: 3 -> 13; matrix products, arithmetic and copies ran while one was open for 3% -> 6% of each run, Pallas kernels for 0% -> 12%
where the time goes in v1:
time: 138 us; the launch traced here: 137 us
  starting transfers between devices  52.5 us (38%)
  waiting for transfers between devices  32.2 us (23%)
  Pallas kernels  32.1 us (23%)
  local copies, waits for them, and re-layouts  8.34 us (6%)
  other arithmetic  8.15 us (6%)
  between operations  4.24 us (3%)
    ppermute x26, starting transfers between devices, send(): return lax.ppermute(value, AXES, pairs)  44 us
    ppermute x26, waiting for transfers between devices, send(): return lax.ppermute(value, AXES, pairs)  27.6 us
    pallas_call x1, Pallas kernels, score(): pl.pallas_call(score_kernel, out_shape=(jax.ShapeDtypeStruct((M, M), BF16...  13.2 us
    all_to_all x1, starting transfers between devices, on_device(): lax.all_to_all(jnp.tile(loss, (NZ, 1)), ('zh', 'zl'), 0, 0, tiled=True)  8.46 us
    unnamed x25, local copies, waits for them, and re-layouts  7.6 us
    pallas_call x1, Pallas kernels, across(): pl.pallas_call(across_kernel, out_shape=(f32(ROWS),) * 3, in_specs=[SMEM]...  7.45 us
    pallas_call x1, Pallas kernels, nearby(): pl.pallas_call(near_kernel, out_shape=(f32(ROWS),) * 2, in_specs=[SMEM] +...  6.77 us
    all_to_all x1, waiting for transfers between devices, on_device(): lax.all_to_all(jnp.tile(loss, (NZ, 1)), ('zh', 'zl'), 0, 0, tiled=True)  4.54 us
  transfers between devices with their start and end apart: 27, of which 13 were waited for; matrix products, arithmetic and copies ran while one was open for 6% of the time, Pallas kernels for 12%

profile of v1, /device:TPU:24, one launch (start us, length us, event | category | flops | bytes accessed | tf_op | source)
XLA Modules:
  0.0 137.4 jit_solution(15167462614886828072)
XLA Ops:
  0.6 2.0 %normalize.1 = (bf16[88,1152]{1,0:T(8,128)(2,1)}, bf16[88,1152]{1,0:T(8,128)(2,1)}) custom-call(f32[88,1152]{1,0:T(8,128)} %img_ref.3, f32[88,1152]{1,0:T(8,128)} %txt_ref.3), custom_call_target="tpu_custom_call" | custom-call | tf_op jit(solution)/shard_map/normalize/pallas_call | solution.py:70
  2.6 3.0 %collective-permute-start.2 = (bf16[88,1152]{1,0:T(8,128)(2,1)}, bf16[88,1152]{1,0:T(8,128)(2,1)S(1)}, u32[]{:S(2)}, u32[]{:S(2)}) collective-permute-start(bf16[88,1152]{1,0:T(8,128)(2,1)} %get-tuple-element.23), channel_id=1, source_target_pairs={{0,16},{32,36},{64,80},{96,100},{128,144},{160,164},{192,208},{224... | collective-permute-start | bytes 608264 | tf_op jit(solution)/shard_map/ppermute | solution.py:59
  5.7 1.1 collective-permute-start.1
  6.8 0.9 collective-permute-start
  7.7 1.0 constant_dynamic-update-slice_fusion.3
  8.7 5.3 %collective-permute-done = bf16[88,1152]{1,0:T(8,128)(2,1)S(1)} collective-permute-done((bf16[88,1152]{1,0:T(8,128)(2,1)}, bf16[88,1152]{1,0:T(8,128)(2,1)S(1)}, u32[]{:S(2)}, u32[]{:S(2)}) %collective-permute-start) | collective-permute-done | bytes 202784 | tf_op jit(solution)/shard_map/ppermute | solution.py:59
  14.1 0.8 collective-permute-start.6
  14.9 5.9 %collective-permute-start.4 = (bf16[88,1152]{1,0:T(8,128)(2,1)S(1)}, bf16[88,1152]{1,0:T(8,128)(2,1)S(1)}, u32[]{:S(2)}, u32[]{:S(2)}) collective-permute-start(bf16[88,1152]{1,0:T(8,128)(2,1)S(1)} %copy-done.10), channel_id=1, source_target_pairs={{0,193},{32,225},{64,0},{96,32},{128,64},{160,96},{192,128},{224,1... | collective-permute-start | bytes 608264 | tf_op jit(solution)/shard_map/ppermute | solution.py:59
  20.7 1.4 %collective-permute-start.5 = (bf16[88,1152]{1,0:T(8,128)(2,1)S(1)}, bf16[88,1152]{1,0:T(8,128)(2,1)S(1)}, u32[]{:S(2)}, u32[]{:S(2)}) collective-permute-start(bf16[88,1152]{1,0:T(8,128)(2,1)S(1)} %copy-done.10), channel_id=1, source_target_pairs={{0,1},{32,33},{64,65},{96,97},{128,129},{160,161},{192,193},{224,2... | collective-permute-start | bytes 608264 | tf_op jit(solution)/shard_map/ppermute | solution.py:59
  22.2 1.9 %collective-permute-start.3 = (bf16[88,1152]{1,0:T(8,128)(2,1)S(1)}, bf16[88,1152]{1,0:T(8,128)(2,1)S(1)}, u32[]{:S(2)}, u32[]{:S(2)}) collective-permute-start(bf16[88,1152]{1,0:T(8,128)(2,1)S(1)} %copy-done.10), channel_id=1, source_target_pairs={{0,64},{32,96},{64,128},{96,160},{128,192},{160,224},{192,1},{224,... | collective-permute-start | bytes 608264 | tf_op jit(solution)/shard_map/ppermute | solution.py:59
  24.1 2.5 %collective-permute-start.7 = (bf16[352,1152]{1,0:T(8,128)(2,1)S(1)}, bf16[352,1152]{1,0:T(8,128)(2,1)S(1)}, u32[]{:S(2)}, u32[]{:S(2)}) collective-permute-start(bf16[352,1152]{1,0:T(8,128)(2,1)S(1)} %constant_dynamic-update-slice_fusion.refs_0_), channel_id=1, source_target_pairs={{0,2},{32,40},{64,66},{96,104},{128,130},{160,168},{192,194},{224,... | collective-permute-start | bytes 2433032 | tf_op jit(solution)/shard_map/ppermute | solution.py:59
  26.6 6.3 %collective-permute-done.4 = bf16[88,1152]{1,0:T(8,128)(2,1)S(1)} collective-permute-done((bf16[88,1152]{1,0:T(8,128)(2,1)S(1)}, bf16[88,1152]{1,0:T(8,128)(2,1)S(1)}, u32[]{:S(2)}, u32[]{:S(2)}) %collective-permute-start.4) | collective-permute-done | bytes 202784 | tf_op jit(solution)/shard_map/ppermute | solution.py:59
  32.9 1.4 %collective-permute-start.8 = (bf16[352,1152]{1,0:T(8,128)(2,1)S(1)}, bf16[352,1152]{1,0:T(8,128)(2,1)S(1)}, u32[]{:S(2)}, u32[]{:S(2)}) collective-permute-start(bf16[352,1152]{1,0:T(8,128)(2,1)S(1)} %constant_dynamic-update-slice_fusion.refs_0_), channel_id=1, source_target_pairs={{0,4},{32,48},{64,68},{96,112},{128,132},{160,176},{192,196},{224,... | collective-permute-start | bytes 2433032 | tf_op jit(solution)/shard_map/ppermute | solution.py:59
  35.1 1.7 %collective-permute-start.10 = (bf16[176,1152]{1,0:T(8,128)(2,1)S(1)}, bf16[176,1152]{1,0:T(8,128)(2,1)S(1)}, u32[]{:S(2)}, u32[]{:S(2)}) collective-permute-start(bf16[176,1152]{1,0:T(8,128)(2,1)S(1)} %get-tuple-element.58), channel_id=1, source_target_pairs={{0,64},{32,96},{64,128},{96,160},{128,192},{160,224},{192,1},{224,... | collective-permute-start | bytes 1216520 | tf_op jit(solution)/shard_map/ppermute | solution.py:59
  36.8 1.6 %collective-permute-start.9 = (bf16[176,1152]{1,0:T(8,128)(2,1)S(1)}, bf16[176,1152]{1,0:T(8,128)(2,1)S(1)}, u32[]{:S(2)}, u32[]{:S(2)}) collective-permute-start(bf16[176,1152]{1,0:T(8,128)(2,1)S(1)} %get-tuple-element.59), channel_id=1, source_target_pairs={{0,193},{32,225},{64,0},{96,32},{128,64},{160,96},{192,128},{224,1... | collective-permute-start | bytes 1216520 | tf_op jit(solution)/shard_map/ppermute | solution.py:59
  38.6 8.0 %collective-permute-done.10.refs_6_.refs_5_ = bf16[176,1152]{1,0:T(8,128)(2,1)S(1)} collective-permute-done((bf16[176,1152]{1,0:T(8,128)(2,1)S(1)}, bf16[176,1152]{1,0:T(8,128)(2,1)S(1)}, u32[]{:S(2)}, u32[]{:S(2)}) %collective-permute-start.10) | collective-permute-done | bytes 405536 | tf_op jit(solution)/shard_map/ppermute | solution.py:59
  46.7 0.8 collective-permute-done.9.refs_5_.refs_4_
  49.2 0.8 copy-done.3
  50.0 1.0 copy-done.5
  50.9 13.2 %score.1 = (bf16[1408,1408]{1,0:T(8,128)(2,1)}, f32[712,1152]{1,0:T(8,128)}, f32[176,1152]{1,0:T(8,128)S(1)}, f32[176,1152]{1,0:T(8,128)S(1)}) custom-call(f32[1]{0:T(128)S(6)} %copy.10.sc_ref, f32[1]{0:T(128)S(6)} %copy.11.bi_ref, f32[1]{0:T(128)S(6)} %mul.50.lean_ref, bf16[352,1152]{1,0:T(8,128)(2,1)S(1)} %constant_dynamic-update-slice_fusion.refs_0_, ...), custom_call_target="tpu_custom_call" | custom-call | flops 9135194112 | bytes 19464192 | tf_op jit(solution)/shard_map/score/pallas_call | solution.py:225
  64.1 0.8 collective-permute-start.14
  65.0 1.1 copy-done.1
  66.1 1.1 copy-done.4
  67.2 1.1 copy-done.6
  68.4 7.5 %across.1 = (f32[352,1152]{1,0:T(8,128)}, f32[352,1152]{1,0:T(8,128)}, f32[352,1152]{1,0:T(8,128)}) custom-call(f32[1]{0:T(128)S(6)} %mul.50.lean_ref, bf16[1408,1408]{1,0:T(8,128)(2,1)} %get-tuple-element.38.coef_ref, bf16[352,1152]{1,0:T(8,128)(2,1)S(1)} %collective-permute-done.6.refs_1_.refs_0_, ...), custom_call_target="tpu_custom_call" | custom-call | flops 3425697792 | bytes 12976128 | tf_op jit(solution)/shard_map/across/pallas_call | solution.py:274
  75.8 1.6 %convert_element_type.97 = f16[352,1152]{1,0:T(8,128)(2,1)S(1)} convert(f32[352,1152]{1,0:T(8,128)} %get-tuple-element.33) | non-fusion elementwise | flops 405504 | bytes 2433024 | tf_op jit(solution)/shard_map/convert_element_type | solution.py:378
  77.8 1.1 copy-done.8
  79.3 2.3 %collective-permute-start.22 = (f16[176,1152]{1,0:T(8,128)(2,1)S(1)}, f16[176,1152]{1,0:T(8,128)(2,1)S(1)}, u32[]{:S(2)}, u32[]{:S(2)}) collective-permute-start(f16[176,1152]{1,0:T(8,128)(2,1)S(1)} %get-tuple-element.50), channel_id=1, source_target_pairs={{0,193},{32,225},{64,0},{96,32},{128,64},{160,96},{192,128},{224,1... | collective-permute-start | bytes 1216520 | tf_op jit(solution)/shard_map/ppermute | solution.py:59
  81.6 0.7 multiply_floor_fusion.3
  82.8 1.1 collective-permute-start.15
  83.9 1.0 collective-permute-start.16
  84.9 1.3 collective-permute-start.17
  86.2 6.8 %nearby.1 = (f32[352,1152]{1,0:T(8,128)}, f32[352,1152]{1,0:T(8,128)}) custom-call(f32[1]{0:T(128)S(6)} %mul.50.lean_ref, bf16[1408,1408]{1,0:T(8,128)(2,1)} %get-tuple-element.38.coef_ref, bf16[352,1152]{1,0:T(8,128)(2,1)S(1)} %constant_dynamic-update-slice_fusion.refs_0_, bf16[352,1152]{1,0:T(8,128)(2,1)S(1)} %collective-permute-done.6.refs_1_.refs_0_, ...), custom_call_target="tpu_custom_call" | custom-call | flops 2283798528 | bytes 19464192 | tf_op jit(solution)/shard_map/nearby/pallas_call | solution.py:317
  93.0 1.6 %slice_add_fusion = f32[352,1152]{1,0:T(8,128)S(1)} fusion(f32[352,1152]{1,0:T(8,128)} %get-tuple-element.40, f32[712,1152]{1,0:T(8,128)S(1)} %collective-permute-done.14), kind=kLoop, calls=%fused_computation.2 | loop fusion | flops 405504 | bytes 4866048 | tf_op jit(solution)/shard_map/add | solution.py:413
  94.8 6.5 %collective-permute-start.23 = (f16[88,1152]{1,0:T(8,128)(2,1)S(1)}, f16[88,1152]{1,0:T(8,128)(2,1)S(1)}, u32[]{:S(2)}, u32[]{:S(2)}) collective-permute-start(f16[88,1152]{1,0:T(8,128)(2,1)S(1)} %get-tuple-element.52), channel_id=1, source_target_pairs={{0,1},{32,33},{64,65},{96,97},{128,129},{160,161},{192,193},{224,2... | collective-permute-start | bytes 608264 | tf_op jit(solution)/shard_map/ppermute | solution.py:59
  101.3 3.2 %collective-permute-start.25 = (f16[88,1152]{1,0:T(8,128)(2,1)S(1)}, f16[88,1152]{1,0:T(8,128)(2,1)S(1)}, u32[]{:S(2)}, u32[]{:S(2)}) collective-permute-start(f16[88,1152]{1,0:T(8,128)(2,1)S(1)} %get-tuple-element.53), channel_id=1, source_target_pairs={{0,193},{32,225},{64,0},{96,32},{128,64},{160,96},{192,128},{224,1... | collective-permute-start | bytes 608264 | tf_op jit(solution)/shard_map/ppermute | solution.py:59
  104.5 1.9 %collective-permute-done.16 = f16[360,1152]{1,0:T(8,128)(2,1)S(1)} collective-permute-done((f16[360,1152]{1,0:T(8,128)(2,1)S(1)}, f16[360,1152]{1,0:T(8,128)(2,1)S(1)}, u32[]{:S(2)}, u32[]{:S(2)}) %collective-permute-start.16) | collective-permute-done | bytes 829472 | tf_op jit(solution)/shard_map/ppermute | solution.py:59
  107.3 3.2 %collective-permute-start.19 = (f16[96,1152]{1,0:T(8,128)(2,1)S(1)}, f16[96,1152]{1,0:T(8,128)(2,1)S(1)}, u32[]{:S(2)}, u32[]{:S(2)}) collective-permute-start(f16[96,1152]{1,0:T(8,128)(2,1)S(1)} %get-tuple-element.61), channel_id=1, source_target_pairs={{0,24},{32,38},{64,88},{96,102},{128,152},{160,166},{192,216},{224... | collective-permute-start | bytes 663560 | tf_op jit(solution)/shard_map/ppermute | solution.py:59
  110.5 2.2 %collective-permute-start.20 = (f16[96,1152]{1,0:T(8,128)(2,1)S(1)}, f16[96,1152]{1,0:T(8,128)(2,1)S(1)}, u32[]{:S(2)}, u32[]{:S(2)}) collective-permute-start(f16[96,1152]{1,0:T(8,128)(2,1)S(1)} %get-tuple-element.62), channel_id=1, source_target_pairs={{0,16},{32,36},{64,80},{96,100},{128,144},{160,164},{192,208},{224... | collective-permute-start | bytes 663560 | tf_op jit(solution)/shard_map/ppermute | solution.py:59
  113.2 1.0 collective-permute-done.24
  114.2 0.9 slice_add_fusion.6.gt_ref
  115.0 1.3 collective-permute-done.19
  116.4 1.6 %collective-permute-done.20 = f16[96,1152]{1,0:T(8,128)(2,1)S(1)} collective-permute-done((f16[96,1152]{1,0:T(8,128)(2,1)S(1)}, f16[96,1152]{1,0:T(8,128)(2,1)S(1)}, u32[]{:S(2)}, u32[]{:S(2)}) %collective-permute-start.20) | collective-permute-done | bytes 221216 | tf_op jit(solution)/shard_map/ppermute | solution.py:59
  118.0 0.6 tile.2
  118.6 8.5 %all-to-all-start = ((f32[8,8,128]{2,1,0:T(8,128)}), f32[8,8,128]{2,1,0:T(8,128)S(1)}, u32[]{:S(2)}, u32[]{:S(2)}) async-start(f32[8,8,128]{2,1,0:T(8,128)} %tile.2), calls=%async_computation | async-start | bytes 65536 | tf_op jit(solution)/shard_map/all_to_all | solution.py:426
  127.0 0.9 slice_add_fusion.7.gi_ref
  127.9 2.6 %project.1 = (f32[88,1152]{1,0:T(8,128)}, f32[88,1152]{1,0:T(8,128)}) custom-call(f32[1]{0:T(128)S(6)} %copy.10.sc_ref, f32[1]{0:T(128)S(6)} %mul.50.lean_ref, f32[88,1152]{1,0:T(8,128)} %img_ref.3, f32[88,1152]{1,0:T(8,128)} %txt_ref.3, f32[88,1152]{1,0:T(8,128)} %slice_add_fusion.7.gi_ref, f32[88,1152]{1,0:T(8,128)} %slice_add_fusion.6.gt_ref), custom_call_target="tpu_custom_call" | custom-call | tf_op jit(solution)/shard_map/project/pallas_call | solution.py:92
  130.5 4.5 %all-to-all-done = f32[8,8,128]{2,1,0:T(8,128)S(1)} async-done(((f32[8,8,128]{2,1,0:T(8,128)}), f32[8,8,128]{2,1,0:T(8,128)S(1)}, u32[]{:S(2)}, u32[]{:S(2)}) %all-to-all-start) | async-done | bytes 32800 | tf_op jit(solution)/shard_map/all_to_all | solution.py:426
  (61 shorter events, 4.6 us)
Async XLA Ops:
  2.6 12.3 %copy-start.10 = (bf16[88,1152]{1,0:T(8,128)(2,1)S(1)}, bf16[88,1152]{1,0:T(8,128)(2,1)}, u32[]{:S(2)}) copy-start(bf16[88,1152]{1,0:T(8,128)(2,1)} %get-tuple-element.26) | copy-start | bytes 608260
  2.6 11.4 %collective-permute-start.2 = (bf16[88,1152]{1,0:T(8,128)(2,1)}, bf16[88,1152]{1,0:T(8,128)(2,1)S(1)}, u32[]{:S(2)}, u32[]{:S(2)}) collective-permute-start(bf16[88,1152]{1,0:T(8,128)(2,1)} %get-tuple-element.23), channel_id=1, source_target_pairs={{0,16},{32,36},{64,80},{96,100},{128,144},{160,164},{192,208},{224... | collective-permute-start | bytes 608264 | tf_op jit(solution)/shard_map/ppermute | solution.py:59
  5.7 8.3 %collective-permute-start.1 = (bf16[88,1152]{1,0:T(8,128)(2,1)}, bf16[88,1152]{1,0:T(8,128)(2,1)S(1)}, u32[]{:S(2)}, u32[]{:S(2)}) collective-permute-start(bf16[88,1152]{1,0:T(8,128)(2,1)} %get-tuple-element.23), channel_id=1, source_target_pairs={{0,24},{32,38},{64,88},{96,102},{128,152},{160,166},{192,216},{224... | collective-permute-start | bytes 608264 | tf_op jit(solution)/shard_map/ppermute | solution.py:59
  6.8 7.2 %collective-permute-start = (bf16[88,1152]{1,0:T(8,128)(2,1)}, bf16[88,1152]{1,0:T(8,128)(2,1)S(1)}, u32[]{:S(2)}, u32[]{:S(2)}) collective-permute-start(bf16[88,1152]{1,0:T(8,128)(2,1)} %get-tuple-element.23), channel_id=1, source_target_pairs={{0,8},{32,34},{64,72},{96,98},{128,136},{160,162},{192,200},{224,2... | collective-permute-start | bytes 608264 | tf_op jit(solution)/shard_map/ppermute | solution.py:59
  14.1 24.4 %collective-permute-start.6 = (bf16[352,1152]{1,0:T(8,128)(2,1)S(1)}, bf16[352,1152]{1,0:T(8,128)(2,1)S(1)}, u32[]{:S(2)}, u32[]{:S(2)}) collective-permute-start(bf16[352,1152]{1,0:T(8,128)(2,1)S(1)} %constant_dynamic-update-slice_fusion.refs_0_), channel_id=1, source_target_pairs={{0,6},{32,56},{64,70},{96,120},{128,134},{160,184},{192,198},{224,... | collective-permute-start | bytes 2433032 | tf_op jit(solution)/shard_map/ppermute | solution.py:59
  14.9 18.0 %collective-permute-start.4 = (bf16[88,1152]{1,0:T(8,128)(2,1)S(1)}, bf16[88,1152]{1,0:T(8,128)(2,1)S(1)}, u32[]{:S(2)}, u32[]{:S(2)}) collective-permute-start(bf16[88,1152]{1,0:T(8,128)(2,1)S(1)} %copy-done.10), channel_id=1, source_target_pairs={{0,193},{32,225},{64,0},{96,32},{128,64},{160,96},{192,128},{224,1... | collective-permute-start | bytes 608264 | tf_op jit(solution)/shard_map/ppermute | solution.py:59
  20.7 13.8 %collective-permute-start.5 = (bf16[88,1152]{1,0:T(8,128)(2,1)S(1)}, bf16[88,1152]{1,0:T(8,128)(2,1)S(1)}, u32[]{:S(2)}, u32[]{:S(2)}) collective-permute-start(bf16[88,1152]{1,0:T(8,128)(2,1)S(1)} %copy-done.10), channel_id=1, source_target_pairs={{0,1},{32,33},{64,65},{96,97},{128,129},{160,161},{192,193},{224,2... | collective-permute-start | bytes 608264 | tf_op jit(solution)/shard_map/ppermute | solution.py:59
  22.2 12.9 %collective-permute-start.3 = (bf16[88,1152]{1,0:T(8,128)(2,1)S(1)}, bf16[88,1152]{1,0:T(8,128)(2,1)S(1)}, u32[]{:S(2)}, u32[]{:S(2)}) collective-permute-start(bf16[88,1152]{1,0:T(8,128)(2,1)S(1)} %copy-done.10), channel_id=1, source_target_pairs={{0,64},{32,96},{64,128},{96,160},{128,192},{160,224},{192,1},{224,... | collective-permute-start | bytes 608264 | tf_op jit(solution)/shard_map/ppermute | solution.py:59
  24.1 24.9 %collective-permute-start.7 = (bf16[352,1152]{1,0:T(8,128)(2,1)S(1)}, bf16[352,1152]{1,0:T(8,128)(2,1)S(1)}, u32[]{:S(2)}, u32[]{:S(2)}) collective-permute-start(bf16[352,1152]{1,0:T(8,128)(2,1)S(1)} %constant_dynamic-update-slice_fusion.refs_0_), channel_id=1, source_target_pairs={{0,2},{32,40},{64,66},{96,104},{128,130},{160,168},{192,194},{224,... | collective-permute-start | bytes 2433032 | tf_op jit(solution)/shard_map/ppermute | solution.py:59
  32.9 16.1 %collective-permute-start.8 = (bf16[352,1152]{1,0:T(8,128)(2,1)S(1)}, bf16[352,1152]{1,0:T(8,128)(2,1)S(1)}, u32[]{:S(2)}, u32[]{:S(2)}) collective-permute-start(bf16[352,1152]{1,0:T(8,128)(2,1)S(1)} %constant_dynamic-update-slice_fusion.refs_0_), channel_id=1, source_target_pairs={{0,4},{32,48},{64,68},{96,112},{128,132},{160,176},{192,196},{224,... | collective-permute-start | bytes 2433032 | tf_op jit(solution)/shard_map/ppermute | solution.py:59
  35.1 11.5 %collective-permute-start.10 = (bf16[176,1152]{1,0:T(8,128)(2,1)S(1)}, bf16[176,1152]{1,0:T(8,128)(2,1)S(1)}, u32[]{:S(2)}, u32[]{:S(2)}) collective-permute-start(bf16[176,1152]{1,0:T(8,128)(2,1)S(1)} %get-tuple-element.58), channel_id=1, source_target_pairs={{0,64},{32,96},{64,128},{96,160},{128,192},{160,224},{192,1},{224,... | collective-permute-start | bytes 1216520 | tf_op jit(solution)/shard_map/ppermute | solution.py:59
  36.8 10.6 %collective-permute-start.9 = (bf16[176,1152]{1,0:T(8,128)(2,1)S(1)}, bf16[176,1152]{1,0:T(8,128)(2,1)S(1)}, u32[]{:S(2)}, u32[]{:S(2)}) collective-permute-start(bf16[176,1152]{1,0:T(8,128)(2,1)S(1)} %get-tuple-element.59), channel_id=1, source_target_pairs={{0,193},{32,225},{64,0},{96,32},{128,64},{160,96},{192,128},{224,1... | collective-permute-start | bytes 1216520 | tf_op jit(solution)/shard_map/ppermute | solution.py:59
  38.5 10.7 %copy-start = (bf16[352,1152]{1,0:T(8,128)(2,1)}, bf16[352,1152]{1,0:T(8,128)(2,1)S(1)}, u32[]{:S(2)}) copy-start(bf16[352,1152]{1,0:T(8,128)(2,1)S(1)} %pad_maximum_fusion.refs_4_.refs_3_) | copy-start | bytes 2433028
  38.5 10.6 %collective-permute-start.11 = (bf16[352,1152]{1,0:T(8,128)(2,1)S(1)}, bf16[352,1152]{1,0:T(8,128)(2,1)S(1)}, u32[]{:S(2)}, u32[]{:S(2)}) collective-permute-start(bf16[352,1152]{1,0:T(8,128)(2,1)S(1)} %pad_maximum_fusion.refs_4_.refs_3_), channel_id=1, source_target_pairs={{0,32},{32,0},{64,96},{96,64},{128,160},{160,128},{192,224},{224,1... | collective-permute-start | bytes 2433032 | tf_op jit(solution)/shard_map/ppermute | solution.py:59
  46.7 2.4 %collective-permute-start.13 = (bf16[176,1152]{1,0:T(8,128)(2,1)S(1)}, bf16[176,1152]{1,0:T(8,128)(2,1)S(1)}, u32[]{:S(2)}, u32[]{:S(2)}) collective-permute-start(bf16[176,1152]{1,0:T(8,128)(2,1)S(1)} %collective-permute-done.10.refs_6_.refs_5_), channel_id=1, source_target_pairs={{0,32},{32,0},{64,96},{96,64},{128,160},{160,128},{192,224},{224,1... | collective-permute-start | bytes 1216520 | tf_op jit(solution)/shard_map/ppermute | solution.py:59
  47.4 1.7 %collective-permute-start.12 = (bf16[176,1152]{1,0:T(8,128)(2,1)S(1)}, bf16[176,1152]{1,0:T(8,128)(2,1)S(1)}, u32[]{:S(2)}, u32[]{:S(2)}) collective-permute-start(bf16[176,1152]{1,0:T(8,128)(2,1)S(1)} %collective-permute-done.9.refs_5_.refs_4_), channel_id=1, source_target_pairs={{0,32},{32,0},{64,96},{96,64},{128,160},{160,128},{192,224},{224,1... | collective-permute-start | bytes 1216520 | tf_op jit(solution)/shard_map/ppermute | solution.py:59
  49.0 1.0 copy-start.3
  49.9 1.0 copy-start.5
  64.1 14.9 %collective-permute-start.14 = (f32[712,1152]{1,0:T(8,128)}, f32[712,1152]{1,0:T(8,128)S(1)}, u32[]{:S(2)}, u32[]{:S(2)}) collective-permute-start(f32[712,1152]{1,0:T(8,128)} %get-tuple-element.31), channel_id=1, source_target_pairs={{0,32},{32,0},{64,96},{96,64},{128,160},{160,128},{192,224},{224,1... | collective-permute-start | bytes 9842696 | tf_op jit(solution)/shard_map/ppermute | solution.py:59
  65.0 1.1 copy-start.1
  66.1 1.1 copy-start.4
  67.2 1.1 copy-start.6
  75.8 1.9 %copy-start.9 = (f32[352,1152]{1,0:T(8,128)S(1)}, f32[352,1152]{1,0:T(8,128)}, u32[]{:S(2)}) copy-start(f32[352,1152]{1,0:T(8,128)} %get-tuple-element.35) | copy-start | bytes 4866052
  77.5 1.5 %copy-start.8 = (f32[352,1152]{1,0:T(8,128)S(1)}, f32[352,1152]{1,0:T(8,128)}, u32[]{:S(2)}) copy-start(f32[352,1152]{1,0:T(8,128)} %get-tuple-element.34) | copy-start | bytes 4866052
  79.3 15.3 %collective-permute-start.22 = (f16[176,1152]{1,0:T(8,128)(2,1)S(1)}, f16[176,1152]{1,0:T(8,128)(2,1)S(1)}, u32[]{:S(2)}, u32[]{:S(2)}) collective-permute-start(f16[176,1152]{1,0:T(8,128)(2,1)S(1)} %get-tuple-element.50), channel_id=1, source_target_pairs={{0,193},{32,225},{64,0},{96,32},{128,64},{160,96},{192,128},{224,1... | collective-permute-start | bytes 1216520 | tf_op jit(solution)/shard_map/ppermute | solution.py:59
  81.6 13.0 %collective-permute-start.21 = (f16[176,1152]{1,0:T(8,128)(2,1)S(1)}, f16[176,1152]{1,0:T(8,128)(2,1)S(1)}, u32[]{:S(2)}, u32[]{:S(2)}) collective-permute-start(f16[176,1152]{1,0:T(8,128)(2,1)S(1)} %get-tuple-element.51), channel_id=1, source_target_pairs={{0,64},{32,96},{64,128},{96,160},{128,192},{160,224},{192,1},{224,... | collective-permute-start | bytes 1216520 | tf_op jit(solution)/shard_map/ppermute | solution.py:59
  82.3 3.9 %copy-start.2 = (bf16[352,1152]{1,0:T(8,128)(2,1)S(1)}, bf16[352,1152]{1,0:T(8,128)(2,1)}, u32[]{:S(2)}) copy-start(bf16[352,1152]{1,0:T(8,128)(2,1)} %copy-done) | copy-start | bytes 2433028
  82.8 21.7 %collective-permute-start.15 = (f16[360,1152]{1,0:T(8,128)(2,1)S(1)}, f16[360,1152]{1,0:T(8,128)(2,1)S(1)}, u32[]{:S(2)}, u32[]{:S(2)}) collective-permute-start(f16[360,1152]{1,0:T(8,128)(2,1)S(1)} %get-tuple-element.63), channel_id=1, source_target_pairs={{0,2},{32,40},{64,66},{96,104},{128,130},{160,168},{192,194},{224,... | collective-permute-start | bytes 2488328 | tf_op jit(solution)/shard_map/ppermute | solution.py:59
  83.9 22.5 %collective-permute-start.16 = (f16[360,1152]{1,0:T(8,128)(2,1)S(1)}, f16[360,1152]{1,0:T(8,128)(2,1)S(1)}, u32[]{:S(2)}, u32[]{:S(2)}) collective-permute-start(f16[360,1152]{1,0:T(8,128)(2,1)S(1)} %get-tuple-element.64), channel_id=1, source_target_pairs={{0,6},{32,56},{64,70},{96,120},{128,134},{160,184},{192,198},{224,... | collective-permute-start | bytes 2488328 | tf_op jit(solution)/shard_map/ppermute | solution.py:59
  84.9 21.5 %collective-permute-start.17 = (f16[360,1152]{1,0:T(8,128)(2,1)S(1)}, f16[360,1152]{1,0:T(8,128)(2,1)S(1)}, u32[]{:S(2)}, u32[]{:S(2)}) collective-permute-start(f16[360,1152]{1,0:T(8,128)(2,1)S(1)} %get-tuple-element.65), channel_id=1, source_target_pairs={{0,4},{32,48},{64,68},{96,112},{128,132},{160,176},{192,196},{224,... | collective-permute-start | bytes 2488328 | tf_op jit(solution)/shard_map/ppermute | solution.py:59
  94.6 11.9 %copy-start.7 = (f32[352,1152]{1,0:T(8,128)S(1)}, f32[352,1152]{1,0:T(8,128)}, u32[]{:S(2)}) copy-start(f32[352,1152]{1,0:T(8,128)} %get-tuple-element.39) | copy-start | bytes 4866052
  94.8 15.7 %collective-permute-start.23 = (f16[88,1152]{1,0:T(8,128)(2,1)S(1)}, f16[88,1152]{1,0:T(8,128)(2,1)S(1)}, u32[]{:S(2)}, u32[]{:S(2)}) collective-permute-start(f16[88,1152]{1,0:T(8,128)(2,1)S(1)} %get-tuple-element.52), channel_id=1, source_target_pairs={{0,1},{32,33},{64,65},{96,97},{128,129},{160,161},{192,193},{224,2... | collective-permute-start | bytes 608264 | tf_op jit(solution)/shard_map/ppermute | solution.py:59
  101.3 11.9 %collective-permute-start.25 = (f16[88,1152]{1,0:T(8,128)(2,1)S(1)}, f16[88,1152]{1,0:T(8,128)(2,1)S(1)}, u32[]{:S(2)}, u32[]{:S(2)}) collective-permute-start(f16[88,1152]{1,0:T(8,128)(2,1)S(1)} %get-tuple-element.53), channel_id=1, source_target_pairs={{0,193},{32,225},{64,0},{96,32},{128,64},{160,96},{192,128},{224,1... | collective-permute-start | bytes 608264 | tf_op jit(solution)/shard_map/ppermute | solution.py:59
  104.5 9.6 %collective-permute-start.24 = (f16[88,1152]{1,0:T(8,128)(2,1)S(1)}, f16[88,1152]{1,0:T(8,128)(2,1)S(1)}, u32[]{:S(2)}, u32[]{:S(2)}) collective-permute-start(f16[88,1152]{1,0:T(8,128)(2,1)S(1)} %get-tuple-element.54), channel_id=1, source_target_pairs={{0,64},{32,96},{64,128},{96,160},{128,192},{160,224},{192,1},{224,... | collective-permute-start | bytes 608264 | tf_op jit(solution)/shard_map/ppermute | solution.py:59
  107.2 7.8 %collective-permute-start.18 = (f16[96,1152]{1,0:T(8,128)(2,1)S(1)}, f16[96,1152]{1,0:T(8,128)(2,1)S(1)}, u32[]{:S(2)}, u32[]{:S(2)}) collective-permute-start(f16[96,1152]{1,0:T(8,128)(2,1)S(1)} %get-tuple-element.60), channel_id=1, source_target_pairs={{0,8},{32,34},{64,72},{96,98},{128,136},{160,162},{192,200},{224,2... | collective-permute-start | bytes 663560 | tf_op jit(solution)/shard_map/ppermute | solution.py:59
  107.3 9.1 %collective-permute-start.19 = (f16[96,1152]{1,0:T(8,128)(2,1)S(1)}, f16[96,1152]{1,0:T(8,128)(2,1)S(1)}, u32[]{:S(2)}, u32[]{:S(2)}) collective-permute-start(f16[96,1152]{1,0:T(8,128)(2,1)S(1)} %get-tuple-element.61), channel_id=1, source_target_pairs={{0,24},{32,38},{64,88},{96,102},{128,152},{160,166},{192,216},{224... | collective-permute-start | bytes 663560 | tf_op jit(solution)/shard_map/ppermute | solution.py:59
  110.5 7.4 %collective-permute-start.20 = (f16[96,1152]{1,0:T(8,128)(2,1)S(1)}, f16[96,1152]{1,0:T(8,128)(2,1)S(1)}, u32[]{:S(2)}, u32[]{:S(2)}) collective-permute-start(f16[96,1152]{1,0:T(8,128)(2,1)S(1)} %get-tuple-element.62), channel_id=1, source_target_pairs={{0,16},{32,36},{64,80},{96,100},{128,144},{160,164},{192,208},{224... | collective-permute-start | bytes 663560 | tf_op jit(solution)/shard_map/ppermute | solution.py:59
  118.6 16.5 %all-to-all-start = ((f32[8,8,128]{2,1,0:T(8,128)}), f32[8,8,128]{2,1,0:T(8,128)S(1)}, u32[]{:S(2)}, u32[]{:S(2)}) async-start(f32[8,8,128]{2,1,0:T(8,128)} %tile.2), calls=%async_computation | async-start | bytes 65536 | tf_op jit(solution)/shard_map/all_to_all | solution.py:426
